TPU v7x, 32 devices: a whole 2x2x4 slice. The times are simulated.
32 devices in a mesh: groups: 2 (over x), blk: 16 (over z, y, core).
Axes of the slice: x: 2, y: 2, z: 4, core: 2. Of those that a mesh axis runs over, the one named last changes fastest.
Arguments:
- queries: bfloat16 [32768, 1024], P(('groups', 'blk')), parts along dimension 0, may hold values from -2.5 to 2.5
- passages: bfloat16 [128, 256, 1024], P('blk', 'groups'), parts along dimension 1, may hold values from -12 to 12
- block_list: int32 [256, 4], P(('groups', 'blk')), parts along dimension 0, may hold values from 0 to 127, as said below
- pair_count: int32 [256], P(('groups', 'blk')), parts along dimension 0, may hold values from 1 to 4, 256 in all
- positive: int32 [32768], P(('groups', 'blk')), parts along dimension 0, may hold values from 0 to 511
Outputs:
- row_loss: float32 [32768], P(('groups', 'blk')), parts along dimension 0
- query_grad: bfloat16 [32768, 1024], P(('groups', 'blk')), parts along dimension 0
- passage_grad: bfloat16 [128, 256, 1024], P('blk', 'groups'), parts along dimension 1
There are 2 independent parts, one for each index of `groups`. A program takes and returns all parts, laid end to end along the dimension named above; each array names one. Nothing has to cross between parts.
Inputs may be any that keep to these rules, and one draw needn't show every extreme that they name: `block_list`: each row names 4 different passage blocks; the 8 rows of one index of blk (aligned runs of 8 rows) name exactly 8 different passage blocks in all, each of them in the same number of rows. `pair_count`: the 128 entries of one group sum to 256, and some entry of each group equals 4; the sum holds for each group separately, not over all groups together.
All inputs are finite; a program needn't handle non-finite values.
Results may differ from a plain program's by a relative error of at most 0.0039.
Values may be sent and summed in bfloat16 or wider, within the bound.
A program may use at most 128 MiB of HBM per device.

v0:
```python
import jax
import jax.numpy as jnp
from jax import lax
from jax.sharding import PartitionSpec as P

D = 1024
BLK = 128
NB = 4
DISTINCT = 8


def send_back(partial_value):
    return lax.all_to_all(partial_value, "blk", split_axis=0, concat_axis=1, tiled=True)


def body(queries, passages, block_list, pair_count, positive):
    qblocks_here = block_list.shape[0]
    listed = block_list.reshape(-1)
    pair_total = listed.shape[0]
    span_cols = NB * BLK
    ordered = jnp.sort(listed)
    fresh = jnp.concatenate([jnp.ones((1,), jnp.bool_), ordered[1:] != ordered[:-1]])
    rank_of = jnp.cumsum(fresh.astype(jnp.int32)) - 1
    wanted = jnp.full((DISTINCT,), -1, jnp.int32).at[rank_of].set(ordered)
    matches = listed[:, None] == wanted[None, :]
    slot_index = jnp.sum(
        matches.astype(jnp.int32) * jnp.arange(DISTINCT, dtype=jnp.int32)[None, :], axis=1
    )
    merge_table = matches.astype(jnp.float32)
    requests = lax.all_gather(jnp.maximum(wanted, 0), "blk", axis=0, tiled=True)
    served = passages[:, requests, :]
    fetched = lax.all_to_all(served, "blk", split_axis=1, concat_axis=0, tiled=True)
    candidates = fetched[:, slot_index, :].reshape(BLK, qblocks_here, NB, D)
    query_rows = queries.reshape(qblocks_here, BLK, D)
    scores = jnp.einsum(
        "grd,cgnd->grnc", query_rows, candidates, preferred_element_type=jnp.float32
    )
    scores = scores.reshape(qblocks_here, BLK, span_cols)
    columns = jnp.arange(span_cols, dtype=jnp.int32)
    live_limit = pair_count * BLK
    is_live = columns[None, None, :] < live_limit[:, None, None]
    target_slot = positive.reshape(qblocks_here, BLK) % live_limit[:, None]
    row_max = jnp.max(jnp.where(is_live, scores, -jnp.inf), axis=2, keepdims=True)
    weights = jnp.where(is_live, jnp.exp(scores - row_max), jnp.float32(0.0))
    row_sum = jnp.sum(weights, axis=2, keepdims=True)
    target = jnp.take_along_axis(scores, target_slot[:, :, None], axis=2)[:, :, 0]
    row_loss = row_max[:, :, 0] + jnp.log(row_sum[:, :, 0]) - target
    onehot = (columns[None, None, :] == target_slot[:, :, None]).astype(jnp.float32)
    grad_scores = (
        (weights / row_sum - onehot).astype(jnp.bfloat16).reshape(qblocks_here, BLK, NB, BLK)
    )
    contrib = jnp.einsum(
        "grnc,grd->cgnd", grad_scores, query_rows, preferred_element_type=jnp.float32
    )
    contrib = contrib.reshape(BLK, pair_total, D)
    partial_value = jnp.einsum("cpd,pk->ckd", contrib, merge_table, precision=lax.Precision.HIGHEST)
    query_grad = jnp.einsum(
        "grnc,cgnd->grd", grad_scores, candidates, preferred_element_type=jnp.float32
    ).astype(jnp.bfloat16)
    returned = send_back(partial_value)
    passage_grad = jnp.zeros(passages.shape, jnp.float32).at[:, requests, :].add(returned)
    return (row_loss.reshape(-1), query_grad.reshape(-1, D), passage_grad.astype(jnp.bfloat16))


def solution(mesh):
    return jax.shard_map(
        body,
        mesh=mesh,
        in_specs=(
            P(("groups", "blk"), None),
            P("blk", "groups", None),
            P(("groups", "blk"), None),
            P(("groups", "blk")),
            P(("groups", "blk")),
        ),
        out_specs=(P(("groups", "blk")), P(("groups", "blk"), None), P("blk", "groups", None)),
        check_vma=False,
    )
```

profile of v0, /device:TPU:19, one launch (start us, length us, event | category | flops | bytes accessed | tf_op | source)
XLA Modules:
  0.0 248.7 jit_solution(7454822869387522437)
XLA Ops:
  0.7 0.9 copy.39
  1.6 1.6 sort.15
  3.7 1.2 dynamic-slice
  6.4 7.6 %all-reduce = s32[128]{0:T(128)S(1)} all-reduce(s32[128]{0:T(128)S(1)} %maximum_dynamic-update-slice_fusion), channel_id=1, replica_groups=mesh['groups'=2,'blk'=16] {'blk'}, use_global_device_ids=true, to_apply=%add | all-reduce | flops 128 | bytes 1024
  14.0 7.8 %gather_fusion = bf16[128,8,1024]{2,0,1:T(8,128)(2,1)} fusion(bf16[8,128,1024]{2,1,0:T(8,128)(2,1)} %param.6, s32[1024]{0:T(1024)S(1)} %pad_clamp_fusion.1), kind=kCustom, calls=%fused_computation | custom fusion | bytes 4194816 | tf_op jit(solution)/shard_map/gather | solution.py:31
  21.8 4.1 %copy.41 = bf16[8,128,1024]{2,0,1:T(8,128)(2,1)} copy(bf16[8,128,1024]{2,1,0:T(8,128)(2,1)} %bitcast.88) | data formatting | bytes 4194304 | tf_op jit(solution)/shard_map/gather | solution.py:31
  25.8 9.6 %all-to-all-start = ((bf16[8,128,1024]{2,0,1:T(8,128)(2,1)}), bf16[8,128,1024]{2,0,1:T(8,128)(2,1)}, u32[]{:S(2)}, u32[]{:S(2)}) async-start(bf16[8,128,1024]{2,0,1:T(8,128)(2,1)} %copy.41), calls=%async_computation | async-start | bytes 4194304 | tf_op jit(solution)/shard_map/all_to_all | solution.py:32
  36.1 46.6 %all-to-all-done = bf16[8,128,1024]{2,0,1:T(8,128)(2,1)} async-done(((bf16[8,128,1024]{2,0,1:T(8,128)(2,1)}), bf16[8,128,1024]{2,0,1:T(8,128)(2,1)}, u32[]{:S(2)}, u32[]{:S(2)}) %all-to-all-start) | async-done | bytes 2097184 | tf_op jit(solution)/shard_map/all_to_all | solution.py:32
  82.7 3.0 %copy.43 = bf16[16,8,8,1024]{3,2,1,0:T(8,128)(2,1)S(1)} copy(bf16[16,8,8,1024]{3,1,2,0:T(8,128)(2,1)} %bitcast.5) | data formatting | bytes 4194304 | tf_op jit(solution)/shard_map/all_to_all | solution.py:32
  85.7 2.5 copy.47
  88.2 6.6 %gather_fusion.1 = bf16[32,128,1024]{2,1,0:T(8,128)(2,1)} fusion(bf16[128,8,1024]{2,0,1:T(8,128)(2,1)} %copy.47, s32[1024]{0:T(1024)S(1)} %pad_clamp_fusion), kind=kCustom, calls=%fused_computation.1 | custom fusion | bytes 16777344 | tf_op jit(solution)/shard_map/gather | solution.py:33
  94.8 4.8 %fusion.5 = (f32[8,128]{1,0:T(8,128)S(1)}, f32[8,128,4,128]{3,1,2,0:T(8,128)S(1)}) fusion(pred[8,4,128]{2,1,0:T(4,128)(4,1)S(1)} %broadcast_compare_fusion, bf16[128,8,4,1024]{3,0,2,1:T(8,128)(2,1)} %bitcast.85, bf16[8,128,1024,1]{2,1,3,0:T(8,128)(2,1)S(1)} %bitcast.80), kind=kOutput, calls=%fused_computation.11 | convolution fusion | flops 1074789376 | bytes 12591104 | tf_op jit(solution)/shard_map/grd,cgnd->grnc/dot_general | solution.py:35
  100.3 2.5 fusion.23
  102.8 13.3 %fusion.2 = f32[128,8,1024]{2,1,0:T(8,128)} fusion(f32[128,32,1024]{2,0,1:T(8,128)S(1)} %bitcast.82, s32[32]{0:T(128)S(1)} %reshape.340, s32[8]{0:T(128)S(1)} %scatter_custom_fusion), kind=kOutput, calls=%fused_computation.8 | convolution fusion | flops 402653440 | bytes 20971680 | tf_op jit(solution)/shard_map/cpd,pk->ckd/dot_general | solution.py:56
  116.1 5.1 %all-to-all-start.1 = ((f32[128,8,1024]{2,1,0:T(8,128)}), f32[128,8,1024]{2,1,0:T(8,128)}, u32[]{:S(2)}, u32[]{:S(2)}) async-start(f32[128,8,1024]{2,1,0:T(8,128)} %fusion.2), calls=%async_computation.1 | async-start | bytes 8388608 | tf_op jit(solution)/shard_map/all_to_all | solution.py:13
  121.4 15.2 %gather_fusion.2 = f32[1024]{0:T(1024)S(1)} fusion(f32[8,128,512]{1,2,0:T(8,128)} %bitcast.83, s32[1024]{0:T(1024)S(1)} %fusion.14), kind=kCustom, calls=%fused_computation.2 | custom fusion | bytes 20480 | tf_op jit(solution)/shard_map/jit(take_along_axis)/gather | solution.py:46
  136.7 0.7 bitcast_subtract_fusion.1
  137.4 7.3 %bitcast_convert_fusion = bf16[8,128,1024]{2,1,0:T(8,128)(2,1)} fusion(bf16[128,8,4,1024]{3,0,2,1:T(8,128)(2,1)} %bitcast.86, f32[8,128,4,128]{3,1,2,0:T(8,128)} %copy-done.1, s32[8,128]{1,0:T(8,128)S(1)} %add_select_fusion, s32[4,128]{1,0:T(4,128)S(1)} %multiply_add_fusion, f32[8,128]{1,0:T(8,128)S(1)} %fusion.8, f32[8,128]{1,0:T(8,128)S(1)} %get-tuple-element.20, ...), kind=kOutput, calls=%fused_computation.7 | convolution fusion | flops 1078460416 | bytes 12601344 | tf_op jit(solution)/shard_map/grnc,cgnd->grd/dot_general | solution.py:57
  144.7 68.6 %all-to-all-done.1 = f32[128,8,1024]{2,1,0:T(8,128)} async-done(((f32[128,8,1024]{2,1,0:T(8,128)}), f32[128,8,1024]{2,1,0:T(8,128)}, u32[]{:S(2)}, u32[]{:S(2)}) %all-to-all-start.1) | async-done | bytes 4194336 | tf_op jit(solution)/shard_map/all_to_all | solution.py:13
  213.4 7.7 %copy.50 = f32[8,16,8,1024]{3,0,2,1:T(8,128)} copy(f32[8,16,8,1024]{3,2,0,1:T(8,128)} %bitcast.33) | data formatting | bytes 8388608 | tf_op jit(solution)/shard_map/all_to_all | solution.py:13
  221.0 2.5 %broadcast_in_dim.50 = f32[8,128,1024]{2,0,1:T(8,128)} broadcast(f32[]{:T(128)} %constant.47.clone.1), dimensions={} | broadcast | bytes 4194308 | tf_op jit(solution)/shard_map/broadcast_in_dim | solution.py:61
  223.5 20.2 %scatter_fusion = f32[8,128,1024]{2,0,1:T(8,128)} fusion(f32[8,128,1024]{2,0,1:T(8,128)} %broadcast_in_dim.50, s32[128]{0:T(128)S(1)} %compare_select_fusion.6, f32[128,8,1024]{2,1,0:T(8,128)} %bitcast.84), kind=kCustom, calls=%fused_computation.4 | custom fusion | flops 1048576 | bytes 12583424 | tf_op jit(solution)/shard_map/scatter-add | solution.py:61
  243.7 2.5 %convert_element_type.30 = bf16[8,128,1024]{2,0,1:T(8,128)(2,1)S(1)} convert(f32[8,128,1024]{2,0,1:T(8,128)} %scatter_fusion) | non-fusion elementwise | flops 1048576 | bytes 6291456 | tf_op jit(solution)/shard_map/convert_element_type | solution.py:62
  246.2 2.5 copy.51
  (36 shorter events, 2.9 us)
Async XLA Ops:
  0.6 94.2 %copy-start = (bf16[1024,1024]{1,0:T(8,128)(2,1)S(1)}, bf16[1024,1024]{1,0:T(8,128)(2,1)}, u32[]{:S(2)}) copy-start(bf16[1024,1024]{1,0:T(8,128)(2,1)} %param.5) | copy-start | bytes 6291460
  25.8 10.0 %copy-start.3 = (s32[8]{0:T(128)S(1)}, s32[8]{0:T(128)}, u32[]{:S(2)}) copy-start(s32[8]{0:T(128)} %param.8) | copy-start | bytes 100
  25.8 10.1 %copy-start.2 = (s32[1024]{0:T(1024)S(1)}, s32[1024]{0:T(1024)}, u32[]{:S(2)}) copy-start(s32[1024]{0:T(1024)} %param.9) | copy-start | bytes 12292
  25.8 56.9 %all-to-all-start = ((bf16[8,128,1024]{2,0,1:T(8,128)(2,1)}), bf16[8,128,1024]{2,0,1:T(8,128)(2,1)}, u32[]{:S(2)}, u32[]{:S(2)}) async-start(bf16[8,128,1024]{2,0,1:T(8,128)(2,1)} %copy.41), calls=%async_computation | async-start | bytes 4194304 | tf_op jit(solution)/shard_map/all_to_all | solution.py:32
  99.6 3.2 %copy-start.1 = (f32[8,128,4,128]{3,1,2,0:T(8,128)}, f32[8,128,4,128]{3,1,2,0:T(8,128)S(1)}, u32[]{:S(2)}) copy-start(f32[8,128,4,128]{3,1,2,0:T(8,128)S(1)} %get-tuple-element.21) | copy-start | bytes 6291460
  116.1 97.3 %all-to-all-start.1 = ((f32[128,8,1024]{2,1,0:T(8,128)}), f32[128,8,1024]{2,1,0:T(8,128)}, u32[]{:S(2)}, u32[]{:S(2)}) async-start(f32[128,8,1024]{2,1,0:T(8,128)} %fusion.2), calls=%async_computation.1 | async-start | bytes 8388608 | tf_op jit(solution)/shard_map/all_to_all | solution.py:13
where the time goes:
time: 250 us; the launch traced here: 249 us
  waiting for transfers between devices  115 us (46%)
  local copies, waits for them, and re-layouts  54.9 us (22%)
  matrix products  27.9 us (11%)
  other arithmetic  26.8 us (11%)
  starting transfers between devices  14.7 us (6%)
  blocking collectives  7.62 us (3%)
    all_to_all x1, waiting for transfers between devices, send_back(): lax.all_to_all(partial_value, 'blk', split_axis=0, concat_axis=1, tiled=T...  68.6 us
    all_to_all x1, waiting for transfers between devices, body(): lax.all_to_all(served, 'blk', split_axis=1, concat_axis=0, tiled=True)  46.6 us
    scatter-add x1, other arithmetic, body(): jnp.zeros(passages.shape, jnp.float32).at[:, requests, :].add(returned)  20.2 us
    gather x1, local copies, waits for them, and re-layouts, body(): jnp.take_along_axis(scores, target_slot[:, :, None], axis=2)[:, :, 0]  15.2 us
    dot_general x1, matrix products, body(): jnp.einsum('cpd,pk->ckd', contrib, merge_table, precision=lax.Precision.H...  13.3 us
    gather x2, local copies, waits for them, and re-layouts, body(): served = passages[:, requests, :]  11.9 us
    all_to_all x1, starting transfers between devices, body(): lax.all_to_all(served, 'blk', split_axis=1, concat_axis=0, tiled=True)  9.65 us
    all_to_all x1, local copies, waits for them, and re-layouts, send_back(): lax.all_to_all(partial_value, 'blk', split_axis=0, concat_axis=1, tiled=T...  7.69 us
  transfers between devices with their start and end apart: 2, of which 2 were waited for; matrix products, arithmetic and copies ran while one was open for 10% of the time, Pallas kernels for 0%

commit v1 on v0

v1 whole, which is shorter than its diff:
```python
import functools
import jax
import jax.numpy as jnp
from jax import lax
from jax.experimental import pallas as pl
from jax.experimental.pallas import tpu as pltpu
from jax.sharding import PartitionSpec as P

BLK = 128
NB = 4
DISTINCT = 8
F32 = jnp.float32
BF16 = jnp.bfloat16
NT = (((1,), (1,)), ((), ()))
TN = (((0,), (0,)), ((), ()))
TILE = 256
FAR = 3.0e38


def dot(a, b, dims=(((1,), (0,)), ((), ()))):
    return lax.dot_general(a, b, dims, preferred_element_type=F32)


def tiles(length, step):
    def over(body):
        def one(i, carry):
            body(pl.ds(pl.multiple_of(i * step, step), step))
            return carry

        lax.fori_loop(0, length // step, one, 0)

    return over


def kernel(
    n,
    q_hbm, p_hbm, bl, pc, pos,
    loss, qg_hbm, pg_hbm,
    q, p, wsend, wrecv, hot, send, recv, s, g, rsend, rrecv, acc, qg, pg, live, tgt, m8, t8,
    in_sem, own_sem, out_sem, w_s, w_r, f_s, f_r, r_s, r_r,
):
    rows, width = q.shape
    held = p.shape[0]
    pb = wsend.shape[1]
    r_here = held // pb
    mrows = r_here * DISTINCT
    qblocks = rows // BLK
    per = max(1, TILE // mrows)
    groups = list(reversed(range(n // per)))
    me = lax.axis_index("blk")

    def peer(x):
        out, bit = me, 1
        while bit < n:
            if x & bit:
                out = out + bit - 2 * bit * (lax.rem(lax.div(me, bit), 2))
            bit *= 2
        return out

    def remote(src, dst, ss, rs, x):
        return pltpu.make_async_remote_copy(
            src_ref=src, dst_ref=dst, send_sem=ss.at[x], recv_sem=rs.at[x],
            device_id={"blk": peer(x)}, device_id_type=pl.DeviceIdType.MESH,
        )

    def slot(ref, x):
        return ref.at[pl.ds(x * mrows, mrows)]

    def members(grp):
        return [x for x in range(grp * per, (grp + 1) * per)]

    def w_copy(x):
        return remote(wsend, wrecv.at[pl.ds(x * DISTINCT, DISTINCT)], w_s, w_r, x)

    def f_copy(x):
        return remote(slot(send, x), slot(recv, x), f_s, f_r, x)

    def r_copy(x):
        return remote(slot(rsend, x), slot(rrecv, x), r_s, r_r, x)

    load_q = pltpu.make_async_copy(q_hbm, q, in_sem.at[0])
    load_p = pltpu.make_async_copy(p_hbm, p, in_sem.at[1])
    load_p.start()
    load_q.start()
    barrier = pltpu.get_barrier_semaphore()
    for x in range(1, n):
        pl.semaphore_signal(barrier, inc=1, device_id={"blk": peer(x)}, device_id_type=pl.DeviceIdType.MESH)

    lane = lax.broadcasted_iota(jnp.int32, (DISTINCT, pb), 1)
    sub = lax.broadcasted_iota(jnp.int32, (DISTINCT, pb), 0)
    named = lane < 0
    for k in range(qblocks):
        for j in range(NB):
            named = named | (lane == bl[k, j])
    named = named.astype(F32)
    before = (
        lax.broadcasted_iota(jnp.int32, (pb, pb), 0) < lax.broadcasted_iota(jnp.int32, (pb, pb), 1)
    ).astype(F32).astype(BF16)
    rank = dot(named.astype(BF16), before)
    mine = jnp.where(rank == sub.astype(F32), named, 0.0)
    wsend[...] = mine
    wrecv[pl.ds(0, DISTINCT), :] = mine

    pl.semaphore_wait(barrier, n - 1)
    for grp in groups:
        for x in members(grp):
            if x:
                w_copy(x).start()

    wanted = jnp.sum(mine * lane.astype(F32), axis=1, keepdims=True).astype(jnp.int32)
    for k in range(qblocks):
        at = pl.ds(k * BLK, BLK)
        place = jnp.broadcast_to(pos[pl.ds(k, 1), :], (DISTINCT, BLK))
        count = pc[k]
        nth = lax.shift_right_logical(place, 7)
        for _ in range(NB - 1):
            nth = jnp.where(nth >= count, nth - count, nth)
        row = place & (BLK - 1)
        is_live = jnp.zeros((DISTINCT, BLK), F32)
        target = jnp.full((DISTINCT, BLK), -1, jnp.int32)
        for j in range(NB):
            here = jnp.broadcast_to(wanted, (DISTINCT, BLK)) == bl[k, j]
            is_live = jnp.where(here & (jnp.full((DISTINCT, BLK), j, jnp.int32) < count), 1.0, is_live)
            target = jnp.where(here & (nth == j), row, target)
        live[:, at] = is_live
        tgt[:, at] = target

    load_p.wait()
    wide = lax.broadcasted_iota(jnp.int32, (DISTINCT, held), 1)
    for grp in groups:
        for x in members(grp):
            if x:
                w_copy(x).wait_recv()
            w = wrecv[pl.ds(x * DISTINCT, DISTINCT), :]
            w = jnp.concatenate([w] * r_here, axis=1)
            parts = [
                jnp.where((wide >= r * pb) & (wide < (r + 1) * pb), w, 0.0) for r in range(r_here)
            ]
            hot[pl.ds(x * mrows, mrows), :] = jnp.concatenate(parts, axis=0).astype(BF16)
        at = pl.ds(grp * per * mrows, per * mrows)

        @tiles(width, TILE)
        def _(col):
            send[at, col] = dot(hot[at, :], p[:, col]).astype(BF16)

        for x in members(grp):
            if x:
                f_copy(x).start()
    own = pltpu.make_async_copy(slot(send, 0), slot(recv, 0), own_sem)
    own.start()
    load_q.wait()

    m8[...] = jnp.full(m8.shape, -FAR, F32)
    t8[...] = jnp.zeros(t8.shape, F32)
    for grp in groups:
        for x in members(grp):
            if x:
                f_copy(x).wait_recv()
            else:
                own.wait()
        at = pl.ds(grp * per * mrows, per * mrows)

        @tiles(rows, TILE)
        def _(col):
            part = dot(recv[at, :], q[col, :], NT)
            s[at, col] = part
            cube = part.reshape(per * r_here, DISTINCT, TILE)
            m8[:, col] = jnp.maximum(m8[:, col], jnp.max(cube, axis=0))
            total = t8[:, col]
            want = tgt[:, col]
            for i, x in enumerate(members(grp)):
                base = peer(x) * r_here
                for r in range(r_here):
                    total = total + jnp.where(want == base + r, cube[i * r_here + r], 0.0)
            t8[:, col] = total

    shown = live[...] > 0.0
    top = jnp.max(jnp.where(shown, m8[...], -FAR), axis=0, keepdims=True)
    shift = jnp.where(shown, top, FAR)
    m8[...] = shift

    def weigh(i, total):
        at = pl.ds(pl.multiple_of(i * 64, 64), 64)
        cube = s[at, :].reshape(64 // DISTINCT, DISTINCT, rows)
        e = jnp.exp(cube - m8[...][None])
        s[at, :] = e.reshape(64, rows)
        return total + jnp.sum(e, axis=0)

    total = lax.fori_loop(0, n * mrows // 64, weigh, jnp.zeros((DISTINCT, rows), F32))
    row_sum = jnp.sum(total, axis=0, keepdims=True)
    value = top + jnp.log(row_sum) - jnp.sum(t8[...], axis=0, keepdims=True)
    for k in range(qblocks):
        loss[pl.ds(k, 1), :] = value[:, k * BLK:(k + 1) * BLK]
    t8[...] = jnp.broadcast_to(1.0 / row_sum, t8.shape)

    for grp in groups:
        for x in members(grp):
            base = peer(x) * r_here
            at = pl.ds(x * mrows, mrows)
            cube = s[at, :].reshape(r_here, DISTINCT, rows)
            which = base + lax.broadcasted_iota(jnp.int32, cube.shape, 0)
            one = jnp.where(tgt[...][None] == which, 1.0, 0.0)
            g[at, :] = (cube * t8[...][None] - one).reshape(mrows, rows).astype(BF16)
        at = pl.ds(grp * per * mrows, per * mrows)

        @tiles(width, TILE)
        def _(col):
            rsend[at, col] = dot(g[at, :], q[:, col]).astype(BF16)

        for x in members(grp):
            if x:
                r_copy(x).start()

    @tiles(width, TILE)
    def _(col):
        qg[:, col] = dot(g[...], recv[:, col], TN).astype(BF16)

    store_qg = pltpu.make_async_copy(qg, qg_hbm, out_sem.at[0])
    store_qg.start()

    own = pltpu.make_async_copy(slot(rsend, 0), slot(rrecv, 0), own_sem)
    own.start()
    for grp in groups:
        for x in members(grp):
            if x:
                r_copy(x).wait_recv()
            else:
                own.wait()
        at = pl.ds(grp * per * mrows, per * mrows)

        @tiles(width, TILE)
        def _(col):
            part = dot(hot[at, :], rrecv[at, col], TN)
            if grp != groups[0]:
                part = part + acc[:, col]
            if grp == groups[-1]:
                pg[:, col] = part.astype(BF16)
            else:
                acc[:, col] = part

    store_pg = pltpu.make_async_copy(pg, pg_hbm, out_sem.at[1])
    store_pg.start()
    for x in range(1, n):
        w_copy(x).wait_send()
        f_copy(x).wait_send()
        r_copy(x).wait_send()
    store_qg.wait()
    store_pg.wait()


def body(n, queries, passages, block_list, pair_count, positive):
    rows, width = queries.shape
    r_here, pb, _ = passages.shape
    held = r_here * pb
    total = n * r_here * DISTINCT
    any_space = pl.BlockSpec(memory_space=pl.ANY)
    smem = pl.BlockSpec(memory_space=pltpu.SMEM)
    vmem = pl.BlockSpec(memory_space=pltpu.VMEM)
    dma = pltpu.SemaphoreType.DMA
    loss, query_grad, passage_grad = pl.pallas_call(
        functools.partial(kernel, n),
        out_shape=(
            jax.ShapeDtypeStruct((rows // BLK, BLK), F32),
            jax.ShapeDtypeStruct((rows, width), BF16),
            jax.ShapeDtypeStruct((held, width), BF16),
        ),
        in_specs=[any_space, any_space, smem, smem, vmem],
        out_specs=(vmem, any_space, any_space),
        scratch_shapes=[
            pltpu.VMEM((rows, width), BF16),
            pltpu.VMEM((held, width), BF16),
            pltpu.VMEM((DISTINCT, pb), F32),
            pltpu.VMEM((n * DISTINCT, pb), F32),
            pltpu.VMEM((total, held), BF16),
            pltpu.VMEM((total, width), BF16),
            pltpu.VMEM((total, width), BF16),
            pltpu.VMEM((total, rows), F32),
            pltpu.VMEM((total, rows), BF16),
            pltpu.VMEM((total, width), BF16),
            pltpu.VMEM((total, width), BF16),
            pltpu.VMEM((held, width), F32),
            pltpu.VMEM((rows, width), BF16),
            pltpu.VMEM((held, width), BF16),
            pltpu.VMEM((DISTINCT, rows), F32),
            pltpu.VMEM((DISTINCT, rows), jnp.int32),
            pltpu.VMEM((DISTINCT, rows), F32),
            pltpu.VMEM((DISTINCT, rows), F32),
            dma((2,)),
            dma,
            dma((2,)),
            dma((n,)), dma((n,)), dma((n,)), dma((n,)), dma((n,)), dma((n,)),
        ],
        compiler_params=pltpu.CompilerParams(
            collective_id=0, has_side_effects=True, vmem_limit_bytes=52 * 1024 * 1024
        ),
        cost_estimate=pl.CostEstimate(
            flops=10 * rows * width * total, bytes_accessed=8 * rows * width, transcendentals=total * rows
        ),
    )(
        queries,
        passages.reshape(held, width),
        block_list,
        pair_count,
        positive.reshape(rows // BLK, BLK),
    )
    return loss.reshape(-1), query_grad, passage_grad.reshape(passages.shape)


def solution(mesh):
    return jax.shard_map(
        functools.partial(body, mesh.shape["blk"]),
        mesh=mesh,
        in_specs=(
            P(("groups", "blk"), None),
            P("blk", "groups", None),
            P(("groups", "blk"), None),
            P(("groups", "blk")),
            P(("groups", "blk")),
        ),
        out_specs=(P(("groups", "blk")), P(("groups", "blk"), None), P("blk", "groups", None)),
        check_vma=False,
    )
```

time: 250 us -> 121 us (0.48)
  the two profiles are of different devices: /device:TPU:19 before, /device:TPU:0 now
where the time goes in v1:
time: 121 us
  Pallas kernels  113 us (93%)
  local copies, waits for them, and re-layouts  7.24 us (6%)
    pallas_call x1, Pallas kernels, body(): pl.pallas_call(functools.partial(kernel, n), out_shape=(jax.ShapeDtypeStr...  113 us
    unnamed x10, local copies, waits for them, and re-layouts  7.24 us

profile of v1, /device:TPU:0, one launch (start us, length us, event | category | flops | bytes accessed | tf_op | source)
XLA Modules:
  0.0 120.8 jit_solution(10898355796059786989)
XLA Ops:
  0.6 0.8 copy.8.bl
  1.4 0.0 copy-start
  1.4 0.7 copy-done
  2.1 0.0 copy-start.1
  2.1 0.7 copy-done.1
  2.7 112.9 %shard_map.76 = (f32[8,128]{1,0:T(8,128)S(1)}, bf16[1024,1024]{1,0:T(8,128)(2,1)}, bf16[1024,1024]{1,0:T(8,128)(2,1)}) custom-call(bf16[1024,1024]{1,0:T(8,128)(2,1)} %q_hbm.1, bf16[1024,1024]{1,0:T(8,128)(2,1)} %bitcast.7, s32[8,4]{1,0:T(8,128)S(1)} %copy.8.bl, s32[8]{0:T(128)S(1)} %copy-done.1, s32[8,128]{1,0:T(8,128)S(1)} %bitcast.5), custom_call_target="tpu_custom_call" | custom-call | flops 10737418240 | bytes 8388608 | tf_op jit(solution)/shard_map/pallas_call | solution.py:260
  115.7 0.6 copy.12
  116.3 0.0 copy-start.2
  116.3 3.2 %copy.13 = bf16[1024,1024]{1,0:T(8,128)(2,1)} copy(bf16[1024,1024]{1,0:T(8,128)(2,1)} %get-tuple-element.13) | data formatting | bytes 4194304
  119.5 0.0 copy-done.2
  119.5 1.3 %copy.14 = bf16[8,128,1024]{2,1,0:T(8,128)(2,1)} copy(bf16[8,128,1024]{2,1,0:T(8,128)(2,1)S(1)} %bitcast.6) | data formatting | bytes 4194304
Async XLA Ops:
  1.4 0.7 copy-start
  2.1 0.7 copy-start.1
  116.3 3.2 %copy-start.2 = (bf16[1024,1024]{1,0:T(8,128)(2,1)S(1)}, bf16[1024,1024]{1,0:T(8,128)(2,1)}, u32[]{:S(2)}) copy-start(bf16[1024,1024]{1,0:T(8,128)(2,1)} %get-tuple-element.8) | copy-start | bytes 6291460

commit v2 on v1

--- a/solution.py
+++ b/solution.py
@@ -34,10 +34,10 @@
 
 def kernel(
     n,
-    q_hbm, p_hbm, bl, pc, pos,
-    loss, qg_hbm, pg_hbm,
-    q, p, wsend, wrecv, hot, send, recv, s, g, rsend, rrecv, acc, qg, pg, live, tgt, m8, t8,
-    in_sem, own_sem, out_sem, w_s, w_r, f_s, f_r, r_s, r_r,
+    q_hbm, p_hbm, bl_hbm, pc_hbm, pos_hbm,
+    loss, qg, pg,
+    q, p, bl, pc, pos, wsend, wrecv, hot, send, recv, s, g, rsend, rrecv, acc, live, tgt, m8, t8,
+    in_sem, own_sem, w_s, w_r, f_s, f_r, r_s, r_r,
 ):
     rows, width = q.shape
     held = p.shape[0]
@@ -46,7 +46,10 @@
     mrows = r_here * DISTINCT
     qblocks = rows // BLK
     per = max(1, TILE // mrows)
-    groups = list(reversed(range(n // per)))
+    groups = list(range(n // per))
+    half = n // 2
+    order = [x for i in range(half) for x in (half + i, (i + 1) % half)]
+    place_of = {x: i for i, x in enumerate(order)}
     me = lax.axis_index("blk")
 
     def peer(x):
@@ -64,10 +67,10 @@
         )
 
     def slot(ref, x):
-        return ref.at[pl.ds(x * mrows, mrows)]
+        return ref.at[pl.ds(place_of[x] * mrows, mrows)]
 
     def members(grp):
-        return [x for x in range(grp * per, (grp + 1) * per)]
+        return order[grp * per:(grp + 1) * per]
 
     def w_copy(x):
         return remote(wsend, wrecv.at[pl.ds(x * DISTINCT, DISTINCT)], w_s, w_r, x)
@@ -80,6 +83,12 @@
 
     load_q = pltpu.make_async_copy(q_hbm, q, in_sem.at[0])
     load_p = pltpu.make_async_copy(p_hbm, p, in_sem.at[1])
+    small = [
+        pltpu.make_async_copy(a, b, in_sem.at[2 + i])
+        for i, (a, b) in enumerate(((bl_hbm, bl), (pc_hbm, pc), (pos_hbm, pos)))
+    ]
+    for one in small:
+        one.start()
     load_p.start()
     load_q.start()
     barrier = pltpu.get_barrier_semaphore()
@@ -88,10 +97,11 @@
 
     lane = lax.broadcasted_iota(jnp.int32, (DISTINCT, pb), 1)
     sub = lax.broadcasted_iota(jnp.int32, (DISTINCT, pb), 0)
+    small[0].wait()
     named = lane < 0
     for k in range(qblocks):
         for j in range(NB):
-            named = named | (lane == bl[k, j])
+            named = named | (lane == bl[j, k])
     named = named.astype(F32)
     before = (
         lax.broadcasted_iota(jnp.int32, (pb, pb), 0) < lax.broadcasted_iota(jnp.int32, (pb, pb), 1)
@@ -108,6 +118,8 @@
                 w_copy(x).start()
 
     wanted = jnp.sum(mine * lane.astype(F32), axis=1, keepdims=True).astype(jnp.int32)
+    small[1].wait()
+    small[2].wait()
     for k in range(qblocks):
         at = pl.ds(k * BLK, BLK)
         place = jnp.broadcast_to(pos[pl.ds(k, 1), :], (DISTINCT, BLK))
@@ -119,7 +131,7 @@
         is_live = jnp.zeros((DISTINCT, BLK), F32)
         target = jnp.full((DISTINCT, BLK), -1, jnp.int32)
         for j in range(NB):
-            here = jnp.broadcast_to(wanted, (DISTINCT, BLK)) == bl[k, j]
+            here = jnp.broadcast_to(wanted, (DISTINCT, BLK)) == bl[j, k]
             is_live = jnp.where(here & (jnp.full((DISTINCT, BLK), j, jnp.int32) < count), 1.0, is_live)
             target = jnp.where(here & (nth == j), row, target)
         live[:, at] = is_live
@@ -136,7 +148,7 @@
             parts = [
                 jnp.where((wide >= r * pb) & (wide < (r + 1) * pb), w, 0.0) for r in range(r_here)
             ]
-            hot[pl.ds(x * mrows, mrows), :] = jnp.concatenate(parts, axis=0).astype(BF16)
+            hot[pl.ds(place_of[x] * mrows, mrows), :] = jnp.concatenate(parts, axis=0).astype(BF16)
         at = pl.ds(grp * per * mrows, per * mrows)
 
         @tiles(width, TILE)
@@ -196,7 +208,7 @@
     for grp in groups:
         for x in members(grp):
             base = peer(x) * r_here
-            at = pl.ds(x * mrows, mrows)
+            at = pl.ds(place_of[x] * mrows, mrows)
             cube = s[at, :].reshape(r_here, DISTINCT, rows)
             which = base + lax.broadcasted_iota(jnp.int32, cube.shape, 0)
             one = jnp.where(tgt[...][None] == which, 1.0, 0.0)
@@ -215,8 +227,6 @@
     def _(col):
         qg[:, col] = dot(g[...], recv[:, col], TN).astype(BF16)
 
-    store_qg = pltpu.make_async_copy(qg, qg_hbm, out_sem.at[0])
-    store_qg.start()
 
     own = pltpu.make_async_copy(slot(rsend, 0), slot(rrecv, 0), own_sem)
     own.start()
@@ -238,14 +248,10 @@
             else:
                 acc[:, col] = part
 
-    store_pg = pltpu.make_async_copy(pg, pg_hbm, out_sem.at[1])
-    store_pg.start()
     for x in range(1, n):
         w_copy(x).wait_send()
         f_copy(x).wait_send()
         r_copy(x).wait_send()
-    store_qg.wait()
-    store_pg.wait()
 
 
 def body(n, queries, passages, block_list, pair_count, positive):
@@ -254,21 +260,23 @@
     held = r_here * pb
     total = n * r_here * DISTINCT
     any_space = pl.BlockSpec(memory_space=pl.ANY)
-    smem = pl.BlockSpec(memory_space=pltpu.SMEM)
     vmem = pl.BlockSpec(memory_space=pltpu.VMEM)
     dma = pltpu.SemaphoreType.DMA
     loss, query_grad, passage_grad = pl.pallas_call(
         functools.partial(kernel, n),
         out_shape=(
             jax.ShapeDtypeStruct((rows // BLK, BLK), F32),
-            jax.ShapeDtypeStruct((rows, width), BF16),
-            jax.ShapeDtypeStruct((held, width), BF16),
+            pltpu.VMEM((rows, width), BF16),
+            pltpu.VMEM((held, width), BF16),
         ),
-        in_specs=[any_space, any_space, smem, smem, vmem],
-        out_specs=(vmem, any_space, any_space),
+        in_specs=[any_space] * 5,
+        out_specs=(vmem, vmem, vmem),
         scratch_shapes=[
             pltpu.VMEM((rows, width), BF16),
             pltpu.VMEM((held, width), BF16),
+            pltpu.SMEM(block_list.shape[::-1], jnp.int32),
+            pltpu.SMEM(pair_count.shape, jnp.int32),
+            pltpu.VMEM((rows // BLK, BLK), jnp.int32),
             pltpu.VMEM((DISTINCT, pb), F32),
             pltpu.VMEM((n * DISTINCT, pb), F32),
             pltpu.VMEM((total, held), BF16),
@@ -279,15 +287,12 @@
             pltpu.VMEM((total, width), BF16),
             pltpu.VMEM((total, width), BF16),
             pltpu.VMEM((held, width), F32),
-            pltpu.VMEM((rows, width), BF16),
-            pltpu.VMEM((held, width), BF16),
             pltpu.VMEM((DISTINCT, rows), F32),
             pltpu.VMEM((DISTINCT, rows), jnp.int32),
             pltpu.VMEM((DISTINCT, rows), F32),
             pltpu.VMEM((DISTINCT, rows), F32),
-            dma((2,)),
+            dma((5,)),
             dma,
-            dma((2,)),
             dma((n,)), dma((n,)), dma((n,)), dma((n,)), dma((n,)), dma((n,)),
         ],
         compiler_params=pltpu.CompilerParams(
@@ -299,7 +304,7 @@
     )(
         queries,
         passages.reshape(held, width),
-        block_list,
+        block_list.T,
         pair_count,
         positive.reshape(rows // BLK, BLK),
     )

time: 121 us -> 112 us (0.926)
  the two profiles are of different devices: /device:TPU:0 before, /device:TPU:19 now
where the time goes in v2:
time: 112 us
  Pallas kernels  108 us (96%)
  local copies, waits for them, and re-layouts  3.24 us (3%)
    pallas_call x1, Pallas kernels, body(): pl.pallas_call(functools.partial(kernel, n), out_shape=(jax.ShapeDtypeStr...  108 us
    unnamed x5, local copies, waits for them, and re-layouts  3.24 us

profile of v2, /device:TPU:19, one launch (start us, length us, event | category | flops | bytes accessed | tf_op | source)
XLA Modules:
  0.0 111.9 jit_solution(13018811345550509386)
XLA Ops:
  0.6 108.0 %shard_map.76 = (f32[8,128]{1,0:T(8,128)}, bf16[1024,1024]{1,0:T(8,128)(2,1)S(1)}, bf16[1024,1024]{1,0:T(8,128)(2,1)S(1)}) custom-call(bf16[1024,1024]{1,0:T(8,128)(2,1)} %q_hbm.1, bf16[1024,1024]{1,0:T(8,128)(2,1)} %bitcast.7, s32[4,8]{1,0:T(4,128)} %bitcast.9, s32[8]{0:T(128)} %pc_hbm.1, s32[8,128]{1,0:T(8,128)} %bitcast.8), custom_call_target="tpu_custom_call" | custom-call | flops 10737418240 | bytes 8388608 | tf_op jit(solution)/shard_map/pallas_call | solution.py:265
  108.6 1.3 %copy.11 = bf16[1024,1024]{1,0:T(8,128)(2,1)} copy(bf16[1024,1024]{1,0:T(8,128)(2,1)S(1)} %get-tuple-element.10) | data formatting | bytes 4194304
  109.9 0.0 copy-start
  109.9 1.3 %copy.12 = bf16[8,128,1024]{2,1,0:T(8,128)(2,1)} copy(bf16[8,128,1024]{2,1,0:T(8,128)(2,1)S(1)} %bitcast.5) | data formatting | bytes 4194304
  111.3 0.0 copy-done
  111.3 0.6 copy.13
Async XLA Ops:
  109.9 1.3 %copy-start = (f32[8,128]{1,0:T(8,128)S(1)}, f32[8,128]{1,0:T(8,128)}, u32[]{:S(2)}) copy-start(f32[8,128]{1,0:T(8,128)} %get-tuple-element.6) | copy-start | bytes 12292

commit v3 on v2

--- a/solution.py
+++ b/solution.py
@@ -27,7 +27,7 @@
             body(pl.ds(pl.multiple_of(i * step, step), step))
             return carry
 
-        lax.fori_loop(0, length // step, one, 0)
+        lax.fori_loop(0, length // step, one, 0, unroll=True)
 
     return over
 
@@ -69,8 +69,8 @@
     def slot(ref, x):
         return ref.at[pl.ds(place_of[x] * mrows, mrows)]
 
-    def members(grp):
-        return order[grp * per:(grp + 1) * per]
+    def members(grp, size=per):
+        return order[grp * size:(grp + 1) * size]
 
     def w_copy(x):
         return remote(wsend, wrecv.at[pl.ds(x * DISTINCT, DISTINCT)], w_s, w_r, x)
@@ -138,9 +138,10 @@
         tgt[:, at] = target
 
     load_p.wait()
+    first = max(1, per // 2)
     wide = lax.broadcasted_iota(jnp.int32, (DISTINCT, held), 1)
-    for grp in groups:
-        for x in members(grp):
+    for grp in range(n // first):
+        for x in members(grp, first):
             if x:
                 w_copy(x).wait_recv()
             w = wrecv[pl.ds(x * DISTINCT, DISTINCT), :]
@@ -149,13 +150,13 @@
                 jnp.where((wide >= r * pb) & (wide < (r + 1) * pb), w, 0.0) for r in range(r_here)
             ]
             hot[pl.ds(place_of[x] * mrows, mrows), :] = jnp.concatenate(parts, axis=0).astype(BF16)
-        at = pl.ds(grp * per * mrows, per * mrows)
+        at = pl.ds(grp * first * mrows, first * mrows)
 
         @tiles(width, TILE)
         def _(col):
             send[at, col] = dot(hot[at, :], p[:, col]).astype(BF16)
 
-        for x in members(grp):
+        for x in members(grp, first):
             if x:
                 f_copy(x).start()
     own = pltpu.make_async_copy(slot(send, 0), slot(recv, 0), own_sem)
@@ -205,21 +206,22 @@
         loss[pl.ds(k, 1), :] = value[:, k * BLK:(k + 1) * BLK]
     t8[...] = jnp.broadcast_to(1.0 / row_sum, t8.shape)
 
-    for grp in groups:
-        for x in members(grp):
+    last = max(1, per // 2)
+    for grp in range(n // last):
+        for x in members(grp, last):
             base = peer(x) * r_here
             at = pl.ds(place_of[x] * mrows, mrows)
             cube = s[at, :].reshape(r_here, DISTINCT, rows)
             which = base + lax.broadcasted_iota(jnp.int32, cube.shape, 0)
             one = jnp.where(tgt[...][None] == which, 1.0, 0.0)
             g[at, :] = (cube * t8[...][None] - one).reshape(mrows, rows).astype(BF16)
-        at = pl.ds(grp * per * mrows, per * mrows)
+        at = pl.ds(grp * last * mrows, last * mrows)
 
         @tiles(width, TILE)
         def _(col):
             rsend[at, col] = dot(g[at, :], q[:, col]).astype(BF16)
 
-        for x in members(grp):
+        for x in members(grp, last):
             if x:
                 r_copy(x).start()
 

time: 112 us -> 108 us (0.964)
  Pallas kernels: 108 us -> 104 us
    pallas_call x1, Pallas kernels: 108 us -> 104 us  [body(): pl.pallas_call(functools.partial(kernel, n), out_shape=(jax.ShapeDtypeStr...]
where the time goes in v3:
time: 108 us
  Pallas kernels  104 us (96%)
  local copies, waits for them, and re-layouts  3.24 us (3%)
    pallas_call x1, Pallas kernels, body(): pl.pallas_call(functools.partial(kernel, n), out_shape=(jax.ShapeDtypeStr...  104 us
    unnamed x5, local copies, waits for them, and re-layouts  3.24 us

profile of v3, /device:TPU:19, one launch (start us, length us, event | category | flops | bytes accessed | tf_op | source)
XLA Modules:
  0.0 107.9 jit_solution(5397730799214919444)
XLA Ops:
  0.6 104.0 %shard_map.76 = (f32[8,128]{1,0:T(8,128)}, bf16[1024,1024]{1,0:T(8,128)(2,1)S(1)}, bf16[1024,1024]{1,0:T(8,128)(2,1)S(1)}) custom-call(bf16[1024,1024]{1,0:T(8,128)(2,1)} %q_hbm.1, bf16[1024,1024]{1,0:T(8,128)(2,1)} %bitcast.7, s32[4,8]{1,0:T(4,128)} %bitcast.9, s32[8]{0:T(128)} %pc_hbm.1, s32[8,128]{1,0:T(8,128)} %bitcast.8), custom_call_target="tpu_custom_call" | custom-call | flops 10737418240 | bytes 8388608 | tf_op jit(solution)/shard_map/pallas_call | solution.py:267
  104.7 1.3 %copy.11 = bf16[1024,1024]{1,0:T(8,128)(2,1)} copy(bf16[1024,1024]{1,0:T(8,128)(2,1)S(1)} %get-tuple-element.10) | data formatting | bytes 4194304
  106.0 0.0 copy-start
  106.0 1.3 %copy.12 = bf16[8,128,1024]{2,1,0:T(8,128)(2,1)} copy(bf16[8,128,1024]{2,1,0:T(8,128)(2,1)S(1)} %bitcast.5) | data formatting | bytes 4194304
  107.3 0.0 copy-done
  107.3 0.6 copy.13
Async XLA Ops:
  106.0 1.3 %copy-start = (f32[8,128]{1,0:T(8,128)S(1)}, f32[8,128]{1,0:T(8,128)}, u32[]{:S(2)}) copy-start(f32[8,128]{1,0:T(8,128)} %get-tuple-element.6) | copy-start | bytes 12292
